TPU v7x, 128 devices: a whole 4x4x4 slice. The times are simulated.
128 devices in a mesh: expert: 16 (over z, y_hi, core), dp: 8 (over x, y_lo).
Axes of the slice: x: 4, y: 4 (y_hi: 2, y_lo: 2; y = y_hi * 2 + y_lo), z: 4, core: 2. Of those that a mesh axis runs over, the one named last changes fastest.
Arguments:
- tokens: bfloat16 [16384, 2048], P(('expert', 'dp')), may hold values from -6 to 6
- route_weights: float32 [16384, 2], P(('expert', 'dp')), may hold values from 0.1 to 1
- assignment: int32 [16384, 2], P(('expert', 'dp')), may hold values from 0 to 15, all different within a row; in each aligned block of 128 rows (0 to 127, 128 to 255, ...) at most 32 rows name the same one
- out_grad: bfloat16 [16384, 2048], P(('expert', 'dp')), may hold values from -6 to 6
- weights: bfloat16 [16, 3, 2048, 768], P('expert'), may hold values from -0.125 to 0.125
- first_moment: bfloat16 [16, 3, 2048, 768], P('expert', None, 'dp'), may hold values from -12 to 12
- second_moment: bfloat16 [16, 3, 2048, 768], P('expert', None, 'dp'), may hold values from 1 to 400
- partner: int32 [16], replicated, may hold values from 0 to 15, as said below
Outputs:
- moe_out: bfloat16 [16384, 2048], P(('expert', 'dp'))
- token_grads: bfloat16 [16384, 2048], P(('expert', 'dp'))
- route_grads: float32 [16384, 2], P(('expert', 'dp'))
- new_weights: bfloat16 [16, 3, 2048, 768], P('expert', None, 'dp')
- new_first: bfloat16 [16, 3, 2048, 768], P('expert', None, 'dp')
- new_second: bfloat16 [16, 3, 2048, 768], P('expert', None, 'dp')
Inputs may be any that keep to these rules, and one draw needn't show every extreme that they name: `assignment`: among the tokens of one device (aligned blocks of 128 rows) at most 32 rows name any one expert, and one expert is named by exactly 32 rows in some blocks; a row names 2 different experts. partner[e] is e XOR one nonzero number that is the same for all e, so experts trade slots in pairs.
All inputs are finite; a program needn't handle non-finite values.
Results may differ from a plain program's by a relative error of at most 0.025.
Values may be sent and summed in bfloat16 or wider, within the bound.
A program may use at most 128 MiB of HBM per device.

v0:
```python
import jax
import jax.numpy as jnp
from jax import lax
from jax.sharding import PartitionSpec as P

beta_first = 0.9
beta_second = 0.95
learn_rate = 0.001
weight_decay = 0.1
adam_epsilon = 1e-08
first_fix = 0.9999734386011124
second_fix = 0.994079470779666


def swapped(shard, axis, distance):
    return lax.ppermute(shard, axis, [(i, i ^ 1 << distance) for i in range(lax.axis_size(axis))])


def adamw(weight_piece, first_moment, second_moment, gradient):
    first_new = beta_first * first_moment.astype(jnp.float32) + (1.0 - beta_first) * gradient
    second_new = (
        beta_second * second_moment.astype(jnp.float32) + (1.0 - beta_second) * gradient * gradient
    )
    weight_full = weight_piece.astype(jnp.float32)
    update = (
        first_new / first_fix / (jnp.sqrt(second_new / second_fix) + adam_epsilon)
        + weight_decay * weight_full
    )
    return (
        (weight_full - learn_rate * update).astype(jnp.bfloat16),
        first_new.astype(jnp.bfloat16),
        second_new.astype(jnp.bfloat16),
    )


def relocate(stacked, mask_value, bit_count):
    for bit_index in range(bit_count):
        other = swapped(stacked, "expert", bit_index)
        flagged = jnp.bitwise_and(jnp.right_shift(mask_value, bit_index), 1) == 1
        stacked = jnp.where(flagged, other, stacked)
    return stacked


def per_device(
    tokens, route_weights, assignment, out_grad, weights, first_moment, second_moment, partner
):
    loop_size = lax.axis_size("expert")
    tok_count, topk_count = assignment.shape
    width = tokens.shape[1]
    capacity = 2 * tok_count * topk_count // loop_size
    chosen = assignment.reshape(-1)
    pair_count = chosen.shape[0]
    onehot = (chosen[:, None] == jnp.arange(loop_size, dtype=jnp.int32)[None, :]).astype(jnp.int32)
    ranks = jnp.sum((jnp.cumsum(onehot, axis=0) - onehot) * onehot, axis=1)
    slots = chosen * capacity + ranks
    source = (
        jnp.full((loop_size * capacity,), -1, jnp.int32)
        .at[slots]
        .set(jnp.arange(pair_count, dtype=jnp.int32))
    )
    present = (source >= 0)[:, None]
    safe_pair = jnp.maximum(source, 0)
    token_ids = safe_pair // topk_count
    send_rows = jnp.where(present, tokens[token_ids], jnp.zeros((), jnp.bfloat16)).reshape(
        loop_size, capacity, width
    )
    scaled = (
        route_weights.reshape(-1)[safe_pair][:, None] * out_grad[token_ids].astype(jnp.float32)
    ).astype(jnp.bfloat16)
    send_grads = jnp.where(present, scaled, jnp.zeros((), jnp.bfloat16)).reshape(
        loop_size, capacity, width
    )
    mask_value = partner[0]
    bit_count = loop_size.bit_length() - 1
    share = first_moment.shape[2]
    weight_share = lax.dynamic_slice_in_dim(weights, lax.axis_index("dp") * share, share, 2)
    rows_in = lax.all_to_all(send_rows, "expert", split_axis=0, concat_axis=0, tiled=True)
    rows_flat = rows_in.reshape(-1, width)
    weight = weights[0]
    gate_act = jnp.dot(rows_flat, weight[0], preferred_element_type=jnp.float32)
    up_act = jnp.dot(rows_flat, weight[1], preferred_element_type=jnp.float32)
    sigmoid_gate = jax.nn.sigmoid(gate_act)
    silu_gate = gate_act * sigmoid_gate
    hidden = (silu_gate * up_act).astype(jnp.bfloat16)
    expert_out = jnp.einsum(
        "rf,df->rd", hidden, weight[2], preferred_element_type=jnp.float32
    ).astype(jnp.bfloat16)
    returned_rows = lax.all_to_all(
        expert_out.reshape(loop_size, capacity, width),
        "expert",
        split_axis=0,
        concat_axis=0,
        tiled=True,
    )
    pair_out = (
        returned_rows.reshape(-1, width)[slots]
        .reshape(tok_count, topk_count, width)
        .astype(jnp.float32)
    )
    moe_out = jnp.sum(route_weights[:, :, None] * pair_out, axis=1).astype(jnp.bfloat16)
    route_grads = jnp.sum(out_grad.astype(jnp.float32)[:, None, :] * pair_out, axis=2)
    grads_in = lax.all_to_all(send_grads, "expert", split_axis=0, concat_axis=0, tiled=True)
    grad_flat = grads_in.reshape(-1, width)
    hidden_grad = jnp.dot(grad_flat, weight[2], preferred_element_type=jnp.float32)
    gate_grad = (
        hidden_grad * up_act * sigmoid_gate * (1.0 + gate_act * (1.0 - sigmoid_gate))
    ).astype(jnp.bfloat16)
    up_grad = (hidden_grad * silu_gate).astype(jnp.bfloat16)
    row_grads = (
        jnp.einsum("rf,df->rd", gate_grad, weight[0], preferred_element_type=jnp.float32)
        + jnp.einsum("rf,df->rd", up_grad, weight[1], preferred_element_type=jnp.float32)
    ).astype(jnp.bfloat16)
    back_grads = lax.all_to_all(
        row_grads.reshape(loop_size, capacity, width),
        "expert",
        split_axis=0,
        concat_axis=0,
        tiled=True,
    )
    pair_grads = (
        back_grads.reshape(-1, width)[slots]
        .reshape(tok_count, topk_count, width)
        .astype(jnp.float32)
    )
    token_grads = jnp.sum(pair_grads, axis=1).astype(jnp.bfloat16)
    part_gate = jnp.einsum("rd,rf->df", rows_flat, gate_grad, preferred_element_type=jnp.float32)
    part_up = jnp.einsum("rd,rf->df", rows_flat, up_grad, preferred_element_type=jnp.float32)
    part_down = jnp.einsum("rd,rf->df", grad_flat, hidden, preferred_element_type=jnp.float32)
    partial_grads = (
        jnp.stack([part_gate, part_up, part_down]).astype(jnp.bfloat16).astype(jnp.float32)[None]
    )
    gradient = lax.psum_scatter(
        partial_grads.astype(jnp.bfloat16), "dp", scatter_dimension=2, tiled=True
    ).astype(jnp.float32)
    updated, first_new, second_new = adamw(weight_share, first_moment, second_moment, gradient)
    moved = relocate(jnp.stack([updated, first_new, second_new]), mask_value, bit_count)
    return (moe_out, token_grads, route_grads, moved[0], moved[1], moved[2])


def solution(mesh):
    placed = (
        P(("expert", "dp"), None),
        P(("expert", "dp"), None),
        P(("expert", "dp"), None),
        P(("expert", "dp"), None),
        P("expert", None, None, None),
        P("expert", None, "dp", None),
        P("expert", None, "dp", None),
        P(),
    )
    return jax.shard_map(
        per_device,
        mesh=mesh,
        in_specs=placed,
        out_specs=(
            P(("expert", "dp"), None),
            P(("expert", "dp"), None),
            P(("expert", "dp"), None),
            P("expert", None, "dp", None),
            P("expert", None, "dp", None),
            P("expert", None, "dp", None),
        ),
        check_vma=False,
    )
```

profile of v0, /device:TPU:1, one launch (start us, length us, event | category | flops | bytes accessed | tf_op | source)
XLA Modules:
  0.0 625.0 jit_solution(4792661496842284831)
XLA Ops:
  7.2 0.8 broadcast_multiply_fusion
  8.0 0.8 copy.23
  9.3 0.6 reduce-window.6
  10.2 1.4 scatter_custom_fusion
  11.7 0.8 copy.21
  12.6 3.5 gather_fusion.2
  16.3 2.5 gather_fusion.3
  18.8 3.3 gather_fusion
  22.1 4.4 fusion.32
  26.5 37.5 %all_to_all.20 = bf16[16,32,2048]{2,1,0:T(8,128)(2,1)} all-to-all(bf16[16,32,2048]{2,1,0:T(8,128)(2,1)S(1)} %get-tuple-element.23), channel_id=1, replica_groups=mesh['expert'=16,'dp'=8] {'expert'}, dimensions={0} | all-to-all | bytes 4194304 | tf_op jit(solution)/shard_map/all_to_all | solution.py:102
  64.0 4.7 all-to-all-start
  69.2 5.5 fusion.1
  74.7 22.6 %all-to-all-done = bf16[16,32,2048]{2,1,0:T(8,128)(2,1)S(1)} async-done(((bf16[16,32,2048]{2,1,0:T(8,128)(2,1)}), bf16[16,32,2048]{2,1,0:T(8,128)(2,1)S(1)}, u32[]{:S(2)}, u32[]{:S(2)}) %all-to-all-start) | async-done | bytes 2097184 | tf_op jit(solution)/shard_map/all_to_all | solution.py:77
  97.2 3.8 fusion.7
  101.0 4.4 multiply_convert_fusion.1
  105.5 1.8 fusion.18
  107.3 1.8 fusion.17
  109.2 1.8 fusion.16
  111.1 4.8 pad_maximum_fusion
  115.9 187.0 %reduce-scatter.2.cloned.1.call-done = bf16[1,3,256,768]{3,2,1,0:T(8,128)(2,1)} async-done(((bf16[1,3,2048,768]{3,2,1,0:T(8,128)(2,1)}), bf16[1,3,256,768]{3,2,1,0:T(8,128)(2,1)}) %reduce-scatter.2.cloned.1.call-update) | async-done | bytes 1179664 | tf_op jit(solution)/shard_map/reduce_scatter | solution.py:132
  302.8 4.0 fusion.38
  307.3 0.7 collective-permute-start
  308.0 5.8 collective-permute-done
  313.8 0.5 broadcast_select_fusion
  314.4 2.5 collective-permute-start.1
  316.9 76.8 %collective-permute-done.1 = bf16[3,1,3,256,768]{4,3,2,1,0:T(8,128)(2,1)S(1)} collective-permute-done((bf16[3,1,3,256,768]{4,3,2,1,0:T(8,128)(2,1)S(1)}, bf16[3,1,3,256,768]{4,3,2,1,0:T(8,128)(2,1)S(1)}, u32[]{:S(2)}, u32[]{:S(2)}) %collective-permute-start.1) | collective-permute-done | bytes 3538976 | tf_op jit(solution)/shard_map/ppermute | solution.py:16
  393.7 2.1 broadcast_select_fusion.1
  395.8 1.3 collective-permute-start.2
  397.1 5.1 fusion.13
  402.1 7.8 %all-to-all-start.1 = ((bf16[16,32,2048]{2,1,0:T(8,128)(2,1)}), bf16[16,32,2048]{2,1,0:T(8,128)(2,1)S(1)}, u32[]{:S(2)}, u32[]{:S(2)}) async-start(bf16[16,32,2048]{2,1,0:T(8,128)(2,1)} %bitcast.89), calls=%async_computation.1 | async-start | bytes 4194304 | tf_op jit(solution)/shard_map/all_to_all | solution.py:88
  410.0 74.2 %collective-permute-done.2 = bf16[3,1,3,256,768]{4,3,2,1,0:T(8,128)(2,1)} collective-permute-done((bf16[3,1,3,256,768]{4,3,2,1,0:T(8,128)(2,1)}, bf16[3,1,3,256,768]{4,3,2,1,0:T(8,128)(2,1)}, u32[]{:S(2)}, u32[]{:S(2)}) %collective-permute-start.2) | collective-permute-done | bytes 3538976 | tf_op jit(solution)/shard_map/ppermute | solution.py:16
  484.1 4.2 broadcast_select_fusion.2
  488.4 2.9 collective-permute-start.3
  491.3 3.7 fusion.5
  495.0 5.0 add_convert_fusion
  500.0 0.8 all-to-all-done.1
  500.8 8.2 %all-to-all-start.3 = ((bf16[16,32,2048]{2,1,0:T(8,128)(2,1)}), bf16[16,32,2048]{2,1,0:T(8,128)(2,1)}, u32[]{:S(2)}, u32[]{:S(2)}) async-start(bf16[16,32,2048]{2,1,0:T(8,128)(2,1)} %bitcast.90), calls=%async_computation.3 | async-start | bytes 4194304 | tf_op jit(solution)/shard_map/all_to_all | solution.py:113
  509.0 1.1 convert_element_type.98
  510.2 1.4 gather_fusion.1
  511.5 1.3 reshape.207
  512.9 84.7 %all-to-all-done.3 = bf16[16,32,2048]{2,1,0:T(8,128)(2,1)} async-done(((bf16[16,32,2048]{2,1,0:T(8,128)(2,1)}), bf16[16,32,2048]{2,1,0:T(8,128)(2,1)}, u32[]{:S(2)}, u32[]{:S(2)}) %all-to-all-start.3) | async-done | bytes 2097184 | tf_op jit(solution)/shard_map/all_to_all | solution.py:113
  597.5 4.2 gather_fusion.4
  601.8 1.5 reshape.206
  603.3 6.0 multiply_reduce_fusion
  609.3 0.6 copy.27
  610.0 3.6 reduce_sum.44
  613.6 2.4 broadcast_select_fusion.3
  616.0 1.9 slice_bitcast_fusion
  (52 shorter events, 2.2 us)
Async XLA Ops:
  7.2 11.6 %copy-start = (bf16[128,2048]{1,0:T(8,128)(2,1)S(1)}, bf16[128,2048]{1,0:T(8,128)(2,1)}, u32[]{:S(2)}) copy-start(bf16[128,2048]{1,0:T(8,128)(2,1)} %param.8) | copy-start | bytes 1572868
  7.2 9.1 %copy-start.2 = (bf16[128,2048]{1,0:T(8,128)(2,1)S(1)}, bf16[128,2048]{1,0:T(8,128)(2,1)}, u32[]{:S(2)}) copy-start(bf16[128,2048]{1,0:T(8,128)(2,1)} %param.11) | copy-start | bytes 1572868
  64.0 33.2 %all-to-all-start = ((bf16[16,32,2048]{2,1,0:T(8,128)(2,1)}), bf16[16,32,2048]{2,1,0:T(8,128)(2,1)S(1)}, u32[]{:S(2)}, u32[]{:S(2)}) async-start(bf16[16,32,2048]{2,1,0:T(8,128)(2,1)} %get-tuple-element.24), calls=%async_computation | async-start | bytes 4194304 | tf_op jit(solution)/shard_map/all_to_all | solution.py:77
  68.7 234.2 %reduce-scatter.2.cloned.1.call-start = ((), (), s32[]{:S(2)}) async-start(), calls=%async_computation.5 | async-start | bytes 10616832 | tf_op jit(solution)/shard_map/reduce_scatter | solution.py:132
  97.2 3.8 copy-start.12
  101.0 4.4 copy-start.4
  105.4 1.9 copy-start.13
  105.4 1.9 copy-start.10
  105.5 3.7 copy-start.8
  115.8 187.0 %copy-start.5 = (bf16[1,3,256,768]{3,2,1,0:T(8,128)(2,1)S(1)}, bf16[1,3,256,768]{3,2,1,0:T(8,128)(2,1)}, u32[]{:S(2)}) copy-start(bf16[1,3,256,768]{3,2,1,0:T(8,128)(2,1)} %param.14) | copy-start | bytes 3538948
  115.8 187.0 %copy-start.6 = (bf16[1,3,256,768]{3,2,1,0:T(8,128)(2,1)S(1)}, bf16[1,3,256,768]{3,2,1,0:T(8,128)(2,1)}, u32[]{:S(2)}) copy-start(bf16[1,3,256,768]{3,2,1,0:T(8,128)(2,1)} %param.13) | copy-start | bytes 3538948
  306.8 1.2 copy-start.7
  307.3 6.5 %collective-permute-start = (bf16[3,1,3,256,768]{4,3,2,1,0:T(8,128)(2,1)S(1)}, bf16[3,1,3,256,768]{4,3,2,1,0:T(8,128)(2,1)S(1)}, u32[]{:S(2)}, u32[]{:S(2)}) collective-permute-start(bf16[3,1,3,256,768]{4,3,2,1,0:T(8,128)(2,1)S(1)} %pad_maximum_fusion.1), channel_id=1, source_target_pairs={{0,8},{8,0},{16,24},{24,16},{32,40},{40,32},{48,56},{56,48},{64,72... | collective-permute-start | bytes 10616840 | tf_op jit(solution)/shard_map/ppermute | solution.py:16
  314.4 79.3 %collective-permute-start.1 = (bf16[3,1,3,256,768]{4,3,2,1,0:T(8,128)(2,1)S(1)}, bf16[3,1,3,256,768]{4,3,2,1,0:T(8,128)(2,1)S(1)}, u32[]{:S(2)}, u32[]{:S(2)}) collective-permute-start(bf16[3,1,3,256,768]{4,3,2,1,0:T(8,128)(2,1)S(1)} %broadcast_select_fusion), channel_id=1, source_target_pairs={{0,16},{8,24},{16,0},{24,8},{32,48},{40,56},{48,32},{56,40},{64,80... | collective-permute-start | bytes 10616840 | tf_op jit(solution)/shard_map/ppermute | solution.py:16
  393.7 3.4 copy-start.14
  395.8 88.4 %collective-permute-start.2 = (bf16[3,1,3,256,768]{4,3,2,1,0:T(8,128)(2,1)}, bf16[3,1,3,256,768]{4,3,2,1,0:T(8,128)(2,1)}, u32[]{:S(2)}, u32[]{:S(2)}) collective-permute-start(bf16[3,1,3,256,768]{4,3,2,1,0:T(8,128)(2,1)} %broadcast_select_fusion.1), channel_id=1, source_target_pairs={{0,32},{8,40},{16,48},{24,56},{32,0},{40,8},{48,16},{56,24},{64,96... | collective-permute-start | bytes 10616840 | tf_op jit(solution)/shard_map/ppermute | solution.py:16
  402.1 98.7 %all-to-all-start.1 = ((bf16[16,32,2048]{2,1,0:T(8,128)(2,1)}), bf16[16,32,2048]{2,1,0:T(8,128)(2,1)S(1)}, u32[]{:S(2)}, u32[]{:S(2)}) async-start(bf16[16,32,2048]{2,1,0:T(8,128)(2,1)} %bitcast.89), calls=%async_computation.1 | async-start | bytes 4194304 | tf_op jit(solution)/shard_map/all_to_all | solution.py:88
  484.1 7.1 %copy-start.11 = (bf16[512,768]{1,0:T(8,128)(2,1)S(1)}, bf16[512,768]{1,0:T(8,128)(2,1)}, u32[]{:S(2)}) copy-start(bf16[512,768]{1,0:T(8,128)(2,1)} %copy-done.10) | copy-start | bytes 2359300
  488.4 6.6 %copy-start.9 = (bf16[512,768]{1,0:T(8,128)(2,1)S(1)}, bf16[512,768]{1,0:T(8,128)(2,1)}, u32[]{:S(2)}) copy-start(bf16[512,768]{1,0:T(8,128)(2,1)} %copy-done.8) | copy-start | bytes 2359300
  488.4 125.2 %collective-permute-start.3 = (bf16[3,1,3,256,768]{4,3,2,1,0:T(8,128)(2,1)}, bf16[3,1,3,256,768]{4,3,2,1,0:T(8,128)(2,1)}, u32[]{:S(2)}, u32[]{:S(2)}) collective-permute-start(bf16[3,1,3,256,768]{4,3,2,1,0:T(8,128)(2,1)} %broadcast_select_fusion.2), channel_id=1, source_target_pairs={{0,64},{8,72},{16,80},{24,88},{32,96},{40,104},{48,112},{56,120},{... | collective-permute-start | bytes 10616840 | tf_op jit(solution)/shard_map/ppermute | solution.py:16
  500.8 96.7 %all-to-all-start.3 = ((bf16[16,32,2048]{2,1,0:T(8,128)(2,1)}), bf16[16,32,2048]{2,1,0:T(8,128)(2,1)}, u32[]{:S(2)}, u32[]{:S(2)}) async-start(bf16[16,32,2048]{2,1,0:T(8,128)(2,1)} %bitcast.90), calls=%async_computation.3 | async-start | bytes 4194304 | tf_op jit(solution)/shard_map/all_to_all | solution.py:113
  603.3 6.7 %copy-start.3 = (bf16[128,2,2048]{2,1,0:T(2,128)(2,1)S(1)}, bf16[128,2,2048]{2,1,0:T(2,128)(2,1)}, u32[]{:S(2)}) copy-start(bf16[128,2,2048]{2,1,0:T(2,128)(2,1)} %reshape.206) | copy-start | bytes 3145732
  613.6 4.3 copy-start.1
Sparse Core Ops, SparseCore 0:
  116.0 186.8 reduce-scatter.1
where the time goes:
time: 630 us; the launch traced here: 625 us
  waiting for transfers between devices  452 us (72%)
  blocking collectives  37.5 us (6%)
  other arithmetic  35.2 us (6%)
  matrix products  33 us (5%)
  starting transfers between devices  28.5 us (5%)
  local copies, waits for them, and re-layouts  24.3 us (4%)
  between operations  14.7 us (2%)
    reduce_scatter x1, waiting for transfers between devices, per_device(): lax.psum_scatter(partial_grads.astype(jnp.bfloat16), 'dp', scatter_dimens...  187 us
    ppermute x4, waiting for transfers between devices, swapped(): lax.ppermute(shard, axis, [(i, i ^ 1 << distance) for i in range(lax.axis...  157 us
    all_to_all x1, waiting for transfers between devices, per_device(): lax.all_to_all(row_grads.reshape(loop_size, capacity, width), 'expert', s...  84.7 us
    all_to_all x1, blocking collectives, per_device(): lax.all_to_all(send_grads, 'expert', split_axis=0, concat_axis=0, tiled=T...  37.5 us
    all_to_all x1, waiting for transfers between devices, per_device(): lax.all_to_all(send_rows, 'expert', split_axis=0, concat_axis=0, tiled=True)  22.6 us
  transfers between devices with their start and end apart: 8, of which 7 were waited for; matrix products, arithmetic and copies ran while one was open for 7% of the time, Pallas kernels for 0%

commit v1 on v0

v1 whole, which is shorter than its diff:
```python
import functools

import jax
import jax.numpy as jnp
from jax import lax
from jax.experimental import pallas as pl
from jax.experimental.pallas import tpu as pltpu
from jax.sharding import PartitionSpec as P

beta_first = 0.9
beta_second = 0.95
learn_rate = 0.001
weight_decay = 0.1
adam_epsilon = 1e-08
first_fix = 0.9999734386011124
second_fix = 0.994079470779666

MESH = pl.DeviceIdType.MESH
F32 = jnp.float32
BF16 = jnp.bfloat16
LANES = 128
NZ, NY, NC = 4, 2, 2
NX = 4
PLANE = NY * NC


def dot(a, b, ca=1, cb=0):
    return lax.dot_general(a, b, (((ca,), (cb,)), ((), ())), preferred_element_type=F32)


def pair_slots(assign_ref, capacity):
    tok = assign_ref.shape[0]
    lane = lax.broadcasted_iota(jnp.int32, (tok, LANES), 1)
    named = [(assign_ref[:, k : k + 1] == lane).astype(F32) for k in range(2)]
    below = (
        lax.broadcasted_iota(jnp.int32, (tok, tok), 0)
        > lax.broadcasted_iota(jnp.int32, (tok, tok), 1)
    ).astype(F32)
    earlier = dot(below.astype(BF16), (named[0] + named[1]).astype(BF16))
    return [
        assign_ref[:, k : k + 1] * capacity
        + jnp.sum(earlier * named[k], axis=1, keepdims=True).astype(jnp.int32)
        for k in range(2)
    ]


def rem(a, n):
    return lax.rem(a, jnp.int32(n))


def div(a, n):
    return lax.div(a, jnp.int32(n))


def rows_at(index, size):
    return pl.ds(pl.multiple_of(index * size, size), size)


def expert_coords():
    me = lax.axis_index("expert").astype(jnp.int32)
    return me, div(me, PLANE), rem(div(me, NC), NY), rem(me, NC)


def expert_peers():
    me, z, y, core = expert_coords()
    out = []
    for dz in (2, 1, 3, 0):
        for dy in (1, 0):
            for dc in (0, 1):
                if (dz, dy, dc) != (0, 0, 0):
                    out.append(
                        rem(z + dz, NZ) * PLANE + rem(y + dy, NY) * NC + rem(core + dc, NC)
                    )
    return out


def expert_kernel(
    capacity,
    assign_ref,
    rw_ref,
    tok_ref,
    og_ref,
    w_hbm,
    eo_out,
    rg_out,
    pg_out,
    scaled,
    send_rows,
    send_grads,
    rows_in,
    grads_in,
    w,
    coef_gate,
    coef_up,
    hidden,
    gate_grad,
    up_grad,
    eo,
    rg,
    pg,
    w_sem,
    rows_s,
    rows_r,
    grads_s,
    grads_r,
    out_sem,
):
    me, z, y, core = expert_coords()
    tok, width = tok_ref.shape
    ff = w.shape[2]
    chunk = PLANE * capacity
    peers = expert_peers()
    barrier = pltpu.get_barrier_semaphore()
    for peer in peers:
        pl.semaphore_signal(barrier, inc=1, device_id={"expert": peer}, device_id_type=MESH)
    w_copies = [pltpu.make_async_copy(w_hbm.at[0, p], w.at[p], w_sem.at[p]) for p in range(3)]
    for copy in w_copies:
        copy.start()

    slot = pair_slots(assign_ref, capacity)
    slot_lane = lax.broadcasted_iota(jnp.int32, (tok, chunk), 1)
    for k in range(2):
        scaled[k * tok : (k + 1) * tok, :] = (
            rw_ref[:, k : k + 1] * og_ref[...].astype(F32)
        ).astype(BF16)

    def sent(buffer, target, sems_s, sems_r, peer):
        return pltpu.make_async_remote_copy(
            src_ref=buffer.at[rows_at(peer, capacity)],
            dst_ref=target.at[rows_at(me, capacity)],
            send_sem=sems_s.at[peer],
            recv_sem=sems_r.at[me],
            device_id={"expert": peer},
            device_id_type=MESH,
        )

    def own(buffer, target, sems_r):
        return pltpu.make_async_copy(
            buffer.at[rows_at(me, capacity)], target.at[rows_at(me, capacity)], sems_r.at[me]
        )

    def came(buffer, target, sems_s, sems_r, source):
        return pltpu.make_async_remote_copy(
            src_ref=buffer.at[rows_at(source, capacity)],
            dst_ref=target.at[rows_at(source, capacity)],
            send_sem=sems_s.at[source],
            recv_sem=sems_r.at[source],
            device_id={"expert": source},
            device_id_type=MESH,
        )

    def onehots(plane):
        return [(slot[k] - plane * chunk == slot_lane).astype(F32).astype(BF16) for k in range(2)]

    first = True
    at = 0
    for dz in (2, 1, 3, 0):
        plane = rem(z + dz, NZ)
        hot = onehots(plane)
        send_rows[rows_at(plane, chunk), :] = dot(hot[0] + hot[1], tok_ref[...], 0, 0).astype(BF16)
        if first:
            pl.semaphore_wait(barrier, len(peers))
            first = False
        count = PLANE - (dz == 0)
        for peer in peers[at : at + count]:
            sent(send_rows, rows_in, rows_s, rows_r, peer).start()
        at += count
    own(send_rows, rows_in, rows_r).start()
    at = 0
    for dz in (2, 1, 3, 0):
        plane = rem(z + dz, NZ)
        hot = jnp.concatenate(onehots(plane), axis=0)
        send_grads[rows_at(plane, chunk), :] = dot(hot, scaled[...], 0, 0).astype(BF16)
        count = PLANE - (dz == 0)
        for peer in peers[at : at + count]:
            sent(send_grads, grads_in, grads_s, grads_r, peer).start()
        at += count
    own(send_grads, grads_in, grads_r).start()

    for copy in w_copies:
        copy.wait()

    def plane_of(step):
        half = div(step, 2)
        return rem(z + step + half * (1 - 2 * rem(step, 2)), NZ)

    def forward(step, carry):
        plane = plane_of(step)
        for j in range(PLANE):
            came(send_rows, rows_in, rows_s, rows_r, plane * PLANE + j).wait_recv()
        at_rows = rows_at(plane, chunk)
        rows = rows_in[at_rows, :]
        gate = dot(rows, w[0])
        up = dot(rows, w[1])
        sig = jax.nn.sigmoid(gate)
        silu = gate * sig
        hid = (silu * up).astype(BF16)
        hidden[at_rows, :] = hid
        coef_up[at_rows, :] = silu
        coef_gate[at_rows, :] = up * sig * (1.0 + gate * (1.0 - sig))
        eo[at_rows, :] = dot(hid, w[2], 1, 1).astype(BF16)
        return carry

    lax.fori_loop(0, NZ, forward, 0)
    eo_copy = pltpu.make_async_copy(eo, eo_out, out_sem.at[0])
    eo_copy.start()

    def backward(step, carry):
        plane = plane_of(step)
        for j in range(PLANE):
            came(send_grads, grads_in, grads_s, grads_r, plane * PLANE + j).wait_recv()
        at_rows = rows_at(plane, chunk)
        hidden_grad = dot(grads_in[at_rows, :], w[2])
        gate_grad[at_rows, :] = (hidden_grad * coef_gate[at_rows, :]).astype(BF16)
        up_grad[at_rows, :] = (hidden_grad * coef_up[at_rows, :]).astype(BF16)
        return carry

    lax.fori_loop(0, NZ, backward, 0)

    tile = 256
    pg_copies = []
    for p, (left, right) in enumerate(
        ((rows_in, gate_grad), (rows_in, up_grad), (grads_in, hidden))
    ):

        def weight_tile(j, carry, left=left, right=right, p=p):
            at_cols = rows_at(j, tile)
            pg[p, at_cols, :] = dot(left[:, at_cols], right[...], 0, 0).astype(BF16)
            return carry

        lax.fori_loop(0, width // tile, weight_tile, 0)
        copy = pltpu.make_async_copy(pg.at[p], pg_out.at[p], out_sem.at[1 + p])
        copy.start()
        pg_copies.append(copy)

    def row_tile(j, carry):
        at_cols = rows_at(j, tile)
        rg[:, at_cols] = (
            dot(gate_grad[...], w[0, at_cols, :], 1, 1) + dot(up_grad[...], w[1, at_cols, :], 1, 1)
        ).astype(BF16)
        return carry

    lax.fori_loop(0, width // tile, row_tile, 0)
    rg_copy = pltpu.make_async_copy(rg, rg_out, out_sem.at[4])
    rg_copy.start()
    for peer in peers:
        sent(send_rows, rows_in, rows_s, rows_r, peer).wait_send()
        sent(send_grads, grads_in, grads_s, grads_r, peer).wait_send()
    for copy in (eo_copy, *pg_copies, rg_copy):
        copy.wait()


def reduce_kernel(
    capacity,
    assign_ref,
    rw_ref,
    og_ref,
    eo_hbm,
    rg_hbm,
    pg_hbm,
    w_hbm,
    m_ref,
    v_ref,
    moe_ref,
    tg_ref,
    route_ref,
    new_ref,
    ret_eo,
    ret_rg,
    one_l,
    one_r,
    two_l,
    two_r,
    mine_p,
    mine_m,
    mine,
    sum_p,
    sum_m,
    y_out,
    y_in,
    w_own,
    eo_s,
    eo_r,
    rg_s,
    rg_r,
    x_s,
    x_r,
    y_s,
    y_r,
    loc_sem,
):
    me, z, y, core = expert_coords()
    d = lax.axis_index("dp").astype(jnp.int32)
    x, yl = div(d, 2), rem(d, 2)
    tok, width = og_ref.shape
    half = m_ref.shape[2]
    ff = m_ref.shape[3]
    xp, xm, xo = rem(x + 1, NX), rem(x + NX - 1, NX), rem(x + 2, NX)
    right, left, beside = {"dp": xp * 2 + yl}, {"dp": xm * 2 + yl}, {"dp": x * 2 + 1 - yl}
    peers = expert_peers()
    barrier = pltpu.get_barrier_semaphore()
    for target in [{"expert": peer} for peer in peers] + [right, left, beside]:
        pl.semaphore_signal(barrier, inc=1, device_id=target, device_id_type=MESH)

    def part(p, xx, h):
        return pg_hbm.at[p, rows_at(xx * 2 + h, half)]

    local = []

    def bring(src, dst):
        copy = pltpu.make_async_copy(src, dst, loc_sem.at[len(local)])
        copy.start()
        local.append(copy)

    for p in range(3):
        bring(part(p, xp, 0), mine_p.at[p])
        bring(part(p, xm, 1), mine_m.at[p])
    for p in range(3):
        bring(part(p, x, 0), mine.at[p, 0])
        bring(part(p, x, 1), mine.at[p, 1])
    for p in range(3):
        bring(w_hbm.at[0, p, rows_at(d, half)], w_own.at[p])

    pl.semaphore_wait(barrier, len(peers) + 3)

    def put(src, dst, sems_s, sems_r, index, target):
        return pltpu.make_async_remote_copy(
            src_ref=src,
            dst_ref=dst,
            send_sem=sems_s.at[index],
            recv_sem=sems_r.at[index],
            device_id=target,
            device_id_type=MESH,
        )

    one = [
        (
            put(part(p, xo, 0), one_l.at[p], x_s, x_r, 6 * p, right),
            put(part(p, xo, 1), one_r.at[p], x_s, x_r, 6 * p + 1, left),
        )
        for p in range(3)
    ]
    alone = [
        (
            put(part(p, xp, 1), two_l.at[p, 1], x_s, x_r, 6 * p + 2, right),
            put(part(p, xm, 0), two_r.at[p, 0], x_s, x_r, 6 * p + 3, left),
        )
        for p in range(3)
    ]
    both = [
        (
            put(sum_p.at[p], two_l.at[p, 0], x_s, x_r, 6 * p + 4, right),
            put(sum_m.at[p], two_r.at[p, 1], x_s, x_r, 6 * p + 5, left),
        )
        for p in range(3)
    ]
    across = [put(y_out.at[p], y_in.at[p], y_s, y_r, p, beside) for p in range(3)]
    for p in range(3):
        for copy in one[p]:
            copy.start()

    def returned(source, target, sems_s, sems_r, peer):
        return pltpu.make_async_remote_copy(
            src_ref=source.at[rows_at(peer, capacity)],
            dst_ref=target.at[rows_at(me, capacity)],
            send_sem=sems_s.at[peer],
            recv_sem=sems_r.at[me],
            device_id={"expert": peer},
            device_id_type=MESH,
        )

    def came(source, target, sems_s, sems_r, peer):
        return pltpu.make_async_remote_copy(
            src_ref=source.at[rows_at(peer, capacity)],
            dst_ref=target.at[rows_at(peer, capacity)],
            send_sem=sems_s.at[peer],
            recv_sem=sems_r.at[peer],
            device_id={"expert": peer},
            device_id_type=MESH,
        )

    homes = ((eo_hbm, ret_eo, eo_s, eo_r), (rg_hbm, ret_rg, rg_s, rg_r))
    owns = []
    for source, target, sems_s, sems_r in homes:
        for peer in peers:
            returned(source, target, sems_s, sems_r, peer).start()
        copy = pltpu.make_async_copy(
            source.at[rows_at(me, capacity)], target.at[rows_at(me, capacity)], sems_r.at[me]
        )
        copy.start()
        owns.append(copy)
    for p in range(3):
        for copy in alone[p]:
            copy.start()

    for copy in local:
        copy.wait()
    block = 32
    steps = half // block
    for p in range(3):
        for copy in one[p]:
            copy.wait_recv()

        def add(i, carry, p=p):
            at = rows_at(i, block)
            sum_p[p, at, :] = (mine_p[p, at, :].astype(F32) + one_l[p, at, :].astype(F32)).astype(BF16)
            sum_m[p, at, :] = (mine_m[p, at, :].astype(F32) + one_r[p, at, :].astype(F32)).astype(BF16)
            return carry

        lax.fori_loop(0, steps, add, 0)
        for copy in both[p]:
            copy.start()

    slot = pair_slots(assign_ref, capacity)
    slots = ret_eo.shape[0]
    slot_lane = lax.broadcasted_iota(jnp.int32, (tok, slots), 1)
    hot = [(slot[k] == slot_lane).astype(F32).astype(BF16) for k in range(2)]
    hot_both = jnp.concatenate(hot, axis=0)
    hot_sum = hot[0] + hot[1]
    tile = 512
    rw = [rw_ref[:, k : k + 1] for k in range(2)]
    for peer in peers:
        came(*homes[0], peer).wait_recv()
    owns[0].wait()

    def combine(j, route):
        at = rows_at(j, tile)
        pairs = dot(hot_both, ret_eo[:, at])
        first, second = pairs[:tok], pairs[tok:]
        moe_ref[:, at] = (rw[0] * first + rw[1] * second).astype(BF16)
        grad = og_ref[:, at].astype(F32)
        return (
            route[0] + jnp.sum(grad * first, axis=1, keepdims=True),
            route[1] + jnp.sum(grad * second, axis=1, keepdims=True),
        )

    zero = jnp.zeros((tok, 1), F32)
    route = lax.fori_loop(0, width // tile, combine, (zero, zero))
    route_ref[:, 0:1] = route[0]
    route_ref[:, 1:2] = route[1]
    for peer in peers:
        came(*homes[1], peer).wait_recv()
    owns[1].wait()

    def combine_grads(j, carry):
        at = rows_at(j, tile)
        tg_ref[:, at] = dot(hot_sum, ret_rg[:, at]).astype(BF16)
        return carry

    lax.fori_loop(0, width // tile, combine_grads, 0)

    def total(p, h, at):
        return (
            mine[p, h, at, :].astype(F32)
            + two_l[p, h, at, :].astype(F32)
            + two_r[p, h, at, :].astype(F32)
        )

    for p in range(3):
        for copy in (*alone[p], *both[p]):
            copy.wait_recv()

        def sum_other(i, carry, p=p):
            at = rows_at(i, block)
            y_out[p, at, :] = total(p, 1 - yl, at).astype(BF16)
            return carry

        lax.fori_loop(0, steps, sum_other, 0)
        across[p].start()

    for p in range(3):
        across[p].wait_recv()

        def adamw(i, carry, p=p):
            at = rows_at(i, block)
            grad = total(p, yl, at) + y_in[p, at, :].astype(F32)
            first_new = beta_first * m_ref[0, p, at, :].astype(F32) + (1.0 - beta_first) * grad
            second_new = (
                beta_second * v_ref[0, p, at, :].astype(F32) + (1.0 - beta_second) * grad * grad
            )
            full = w_own[p, at, :].astype(F32)
            update = (
                first_new * (1.0 / first_fix)
                / (jnp.sqrt(second_new * (1.0 / second_fix)) + adam_epsilon)
                + weight_decay * full
            )
            new_ref[0, p, at, :] = (full - learn_rate * update).astype(BF16)
            new_ref[1, p, at, :] = first_new.astype(BF16)
            new_ref[2, p, at, :] = second_new.astype(BF16)
            return carry

        lax.fori_loop(0, steps, adamw, 0)

    for p in range(3):
        for copy in (*one[p], *alone[p], *both[p], across[p]):
            copy.wait_send()
    for source, target, sems_s, sems_r in homes:
        for peer in peers:
            returned(source, target, sems_s, sems_r, peer).wait_send()


def move(mask, stacked, count):
    return lax.ppermute(stacked, "expert", [(i, i ^ mask) for i in range(count)])


def per_device(
    tokens, route_weights, assignment, out_grad, weights, first_moment, second_moment, partner
):
    experts = lax.axis_size("expert")
    tok, topk = assignment.shape
    width = tokens.shape[1]
    capacity = 2 * tok * topk // experts
    slots = experts * capacity
    ff = weights.shape[3]
    half = first_moment.shape[2]
    vmem = pl.BlockSpec(memory_space=pltpu.VMEM)
    anywhere = pl.BlockSpec(memory_space=pl.ANY)
    dma = pltpu.SemaphoreType.DMA
    shape = jax.ShapeDtypeStruct
    eo, rg, pg = pl.pallas_call(
        functools.partial(expert_kernel, capacity),
        out_shape=(
            shape((slots, width), BF16),
            shape((slots, width), BF16),
            shape((3, width, ff), BF16),
        ),
        in_specs=[vmem] * 4 + [anywhere],
        out_specs=(anywhere,) * 3,
        scratch_shapes=[
            pltpu.VMEM((topk * tok, width), BF16),
            pltpu.VMEM((slots, width), BF16),
            pltpu.VMEM((slots, width), BF16),
            pltpu.VMEM((slots, width), BF16),
            pltpu.VMEM((slots, width), BF16),
            pltpu.VMEM((3, width, ff), BF16),
            pltpu.VMEM((slots, ff), F32),
            pltpu.VMEM((slots, ff), F32),
            pltpu.VMEM((slots, ff), BF16),
            pltpu.VMEM((slots, ff), BF16),
            pltpu.VMEM((slots, ff), BF16),
            pltpu.VMEM((slots, width), BF16),
            pltpu.VMEM((slots, width), BF16),
            pltpu.VMEM((3, width, ff), BF16),
            dma((3,)),
            dma((experts,)),
            dma((experts,)),
            dma((experts,)),
            dma((experts,)),
            dma((5,)),
        ],
        compiler_params=pltpu.CompilerParams(
            collective_id=0, has_side_effects=True, vmem_limit_bytes=56 * 2**20
        ),
    )(assignment, route_weights, tokens, out_grad, weights)
    piece = (3, half, ff)
    moe_out, token_grads, route_grads, new = pl.pallas_call(
        functools.partial(reduce_kernel, capacity),
        out_shape=(
            shape((tok, width), BF16),
            shape((tok, width), BF16),
            shape((tok, topk), F32),
            shape((3,) + piece, BF16),
        ),
        in_specs=[vmem] * 3 + [anywhere] * 4 + [vmem] * 2,
        out_specs=(vmem,) * 4,
        scratch_shapes=[
            pltpu.VMEM((slots, width), BF16),
            pltpu.VMEM((slots, width), BF16),
            pltpu.VMEM(piece, BF16),
            pltpu.VMEM(piece, BF16),
            pltpu.VMEM((3, 2, half, ff), BF16),
            pltpu.VMEM((3, 2, half, ff), BF16),
            pltpu.VMEM(piece, BF16),
            pltpu.VMEM(piece, BF16),
            pltpu.VMEM((3, 2, half, ff), BF16),
            pltpu.VMEM(piece, BF16),
            pltpu.VMEM(piece, BF16),
            pltpu.VMEM(piece, BF16),
            pltpu.VMEM(piece, BF16),
            pltpu.VMEM(piece, BF16),
            dma((experts,)),
            dma((experts,)),
            dma((experts,)),
            dma((experts,)),
            dma((18,)),
            dma((18,)),
            dma((3,)),
            dma((3,)),
            dma((15,)),
        ],
        compiler_params=pltpu.CompilerParams(
            collective_id=1, has_side_effects=True, vmem_limit_bytes=56 * 2**20
        ),
    )(assignment, route_weights, out_grad, eo, rg, pg, weights, first_moment, second_moment)
    moved = lax.switch(
        partner[0] - 1,
        [functools.partial(move, mask, count=experts) for mask in range(1, experts)],
        new,
    )
    return (moe_out, token_grads, route_grads, moved[0:1], moved[1:2], moved[2:3])


def solution(mesh):
    placed = (
        P(("expert", "dp"), None),
        P(("expert", "dp"), None),
        P(("expert", "dp"), None),
        P(("expert", "dp"), None),
        P("expert", None, None, None),
        P("expert", None, "dp", None),
        P("expert", None, "dp", None),
        P(),
    )
    return jax.shard_map(
        per_device,
        mesh=mesh,
        in_specs=placed,
        out_specs=(
            P(("expert", "dp"), None),
            P(("expert", "dp"), None),
            P(("expert", "dp"), None),
            P("expert", None, "dp", None),
            P("expert", None, "dp", None),
            P("expert", None, "dp", None),
        ),
        check_vma=False,
    )
```

time: 630 us -> 263 us (0.42)
  waiting for transfers between devices: 452 us -> 76.2 us
  Pallas kernels: 0 us -> 173 us
  blocking collectives: 37.5 us -> 0 us
  other arithmetic: 35.2 us -> 0 us
  matrix products: 33 us -> 0 us
  starting transfers between devices: 28.5 us -> 2.01 us
  local copies, waits for them, and re-layouts: 24.3 us -> 9.65 us
  between operations: 14.7 us -> 1.34 us
    reduce_scatter x1 -> x0, waiting for transfers between devices: 187 us -> none  [per_device(): lax.psum_scatter(partial_grads.astype(jnp.bfloat16), 'dp', scatter_dimens...]
    pallas_call x0 -> x2, Pallas kernels: none -> 173 us  [the longest x1 97.2 us: per_device(): pl.pallas_call(functools.partial(reduce_kernel, capacity), out_shape=(sha...]
    all_to_all x3 -> x0, waiting for transfers between devices: 108 us -> none  [the longest x1 84.7 us: per_device(): lax.all_to_all(row_grads.reshape(loop_size, capacity, width), 'expert', s...]
    ppermute x4 -> x1, waiting for transfers between devices: 157 us -> 76.2 us  [move(): lax.ppermute(stacked, 'expert', [(i, i ^ mask) for i in range(count)])]
    all_to_all x1 -> x0, blocking collectives: 37.5 us -> none  [per_device(): lax.all_to_all(send_grads, 'expert', split_axis=0, concat_axis=0, tiled=T...]
    dot_general x9 -> x0, matrix products: 33 us -> none  [the longest x1 5.49 us: per_device(): jnp.dot(grad_flat, weight[2], preferred_element_type=jnp.float32)]
    all_to_all x3 -> x0, starting transfers between devices: 20.7 us -> none  [the longest x1 8.21 us: per_device(): lax.all_to_all(row_grads.reshape(loop_size, capacity, width), 'expert', s...]
    gather x5 -> x0, local copies, waits for them, and re-layouts: 14.9 us -> none  [the longest x1 4.22 us: per_device(): back_grads.reshape(-1, width)[slots].reshape(tok_count, topk_count, width)]
  transfers between devices with their start and end apart: 8 -> 1, of which waited for: 7 -> 1; matrix products, arithmetic and copies ran while one was open for 7% -> 0% of each run, Pallas kernels for 0% -> 0%
where the time goes in v1:
time: 263 us; the launch traced here: 262 us
  Pallas kernels  173 us (66%)
  waiting for transfers between devices  76.2 us (29%)
  local copies, waits for them, and re-layouts  9.65 us (4%)
    pallas_call x1, Pallas kernels, per_device(): pl.pallas_call(functools.partial(reduce_kernel, capacity), out_shape=(sha...  97.2 us
    ppermute x1, waiting for transfers between devices, move(): lax.ppermute(stacked, 'expert', [(i, i ^ mask) for i in range(count)])  76.2 us
    pallas_call x1, Pallas kernels, per_device(): pl.pallas_call(functools.partial(expert_kernel, capacity), out_shape=(sha...  75.5 us
    unnamed x13, local copies, waits for them, and re-layouts  7.45 us
  transfers between devices with their start and end apart: 1, of which 1 were waited for; matrix products, arithmetic and copies ran while one was open for 0% of the time, Pallas kernels for 0%

profile of v1, /device:TPU:1, one launch (start us, length us, event | category | flops | bytes accessed | tf_op | source)
XLA Modules:
  0.0 262.1 jit_solution(15426761074007326396)
XLA Ops:
  1.3 1.4 copy.17.rw_ref
  2.7 1.4 copy.16.assign_ref
  4.1 75.5 %shard_map.127 = (bf16[512,2048]{1,0:T(8,128)(2,1)}, bf16[512,2048]{1,0:T(8,128)(2,1)}, bf16[3,2048,768]{2,1,0:T(8,128)(2,1)}) custom-call(s32[128,2]{1,0:T(8,128)} %copy.16.assign_ref, f32[128,2]{1,0:T(8,128)} %copy.17.rw_ref, bf16[128,2048]{1,0:T(8,128)(2,1)} %tok_ref.1, bf16[128,2048]{1,0:T(8,128)(2,1)} %og_ref.3, bf16[1,3,2048,768]{3,2,1,0:T(8,128)(2,1)} %w_hbm.3), custom_call_target="tpu_custom_call" | custom-call | tf_op jit(solution)/shard_map/pallas_call | solution.py:520
  79.6 97.2 %shard_map.128 = (bf16[128,2048]{1,0:T(8,128)(2,1)}, bf16[128,2048]{1,0:T(8,128)(2,1)}, f32[128,2]{1,0:T(8,128)}, bf16[3,3,256,768]{3,2,1,0:T(8,128)(2,1)S(1)}) custom-call(s32[128,2]{1,0:T(8,128)} %copy.16.assign_ref, f32[128,2]{1,0:T(8,128)} %copy.17.rw_ref, bf16[128,2048]{1,0:T(8,128)(2,1)} %og_ref.3, bf16[512,2048]{1,0:T(8,128)(2,1)} %get-tuple-element.35.eo_hbm, ...), custom_call_target="tpu_custom_call" | custom-call | tf_op jit(solution)/shard_map/pallas_call | solution.py:556
  176.8 1.5 copy.18
  178.3 80.6 %conditional.1 = (bf16[3,3,256,768]{3,2,1,0:T(8,128)(2,1)}, bf16[1,3,256,768]{3,2,1,0:T(8,128)(2,1)S(1)}, bf16[1,3,256,768]{3,2,1,0:T(8,128)(2,1)S(1)}, bf16[1,3,256,768]{3,2,1,0:T(8,128)(2,1)S(1)}) conditional(s32[]{:T(128)} %bitcast, bf16[3,3,256,768]{3,2,1,0:T(8,128)(2,1)S(1)} %get-tuple-element.41, ...), branch_computations={%region_0.0_spmd, %region_1.0_spmd, %region_2.0_spmd, %region_3.0_... | conditional | bytes 21233736 | solution.py:595
  178.3 2.0 collective-permute-start.1
  180.3 76.2 %collective-permute-done.1 = bf16[3,3,256,768]{3,2,1,0:T(8,128)(2,1)} collective-permute-done((bf16[3,3,256,768]{3,2,1,0:T(8,128)(2,1)S(1)}, bf16[3,3,256,768]{3,2,1,0:T(8,128)(2,1)}, u32[]{:S(2)}, u32[]{:S(2)}) %collective-permute-start.1) | collective-permute-done | bytes 3538976 | tf_op jit(solution)/shard_map/cond/branch_1_fun/ppermute | solution.py:503
  256.5 2.2 fusion.1
  258.9 0.0 copy-start
  258.9 0.0 copy-start.1
  258.9 0.0 copy-start.2
  258.9 0.0 copy-start.3
  258.9 2.3 copy.81
  261.2 0.0 copy-done.3
  261.2 0.8 copy.82
  262.0 0.0 copy-done
  262.0 0.0 copy-done.1
  262.0 0.0 copy-done.2
Async XLA Ops:
  178.3 78.2 %collective-permute-start.1 = (bf16[3,3,256,768]{3,2,1,0:T(8,128)(2,1)S(1)}, bf16[3,3,256,768]{3,2,1,0:T(8,128)(2,1)}, u32[]{:S(2)}, u32[]{:S(2)}) collective-permute-start(bf16[3,3,256,768]{3,2,1,0:T(8,128)(2,1)S(1)} %param.1), channel_id=1, source_target_pairs={{0,16},{8,24},{16,0},{24,8},{32,48},{40,56},{48,32},{56,40},{64,80... | collective-permute-start | bytes 10616840 | tf_op jit(solution)/shard_map/cond/branch_1_fun/ppermute | solution.py:503
  258.9 3.2 %copy-start = (bf16[1,3,256,768]{3,2,1,0:T(8,128)(2,1)}, bf16[1,3,256,768]{3,2,1,0:T(8,128)(2,1)S(1)}, u32[]{:S(2)}) copy-start(bf16[1,3,256,768]{3,2,1,0:T(8,128)(2,1)S(1)} %get-tuple-element.167) | copy-start | bytes 3538948
  258.9 3.2 %copy-start.1 = (bf16[1,3,256,768]{3,2,1,0:T(8,128)(2,1)}, bf16[1,3,256,768]{3,2,1,0:T(8,128)(2,1)S(1)}, u32[]{:S(2)}) copy-start(bf16[1,3,256,768]{3,2,1,0:T(8,128)(2,1)S(1)} %get-tuple-element.166) | copy-start | bytes 3538948
  258.9 3.2 %copy-start.2 = (bf16[1,3,256,768]{3,2,1,0:T(8,128)(2,1)}, bf16[1,3,256,768]{3,2,1,0:T(8,128)(2,1)S(1)}, u32[]{:S(2)}) copy-start(bf16[1,3,256,768]{3,2,1,0:T(8,128)(2,1)S(1)} %get-tuple-element.165) | copy-start | bytes 3538948
  258.9 2.3 copy-start.3

commit v2 on v0

v2 whole, which is shorter than its diff:
```python
import functools

import jax
import jax.numpy as jnp
from jax import lax
from jax.experimental import pallas as pl
from jax.experimental.pallas import tpu as pltpu
from jax.sharding import PartitionSpec as P

beta_first = 0.9
beta_second = 0.95
learn_rate = 0.001
weight_decay = 0.1
adam_epsilon = 1e-08
first_fix = 0.9999734386011124
second_fix = 0.994079470779666

MESH = pl.DeviceIdType.MESH
F32 = jnp.float32
BF16 = jnp.bfloat16
LANES = 128
NZ, NY, NC = 4, 2, 2
NX = 4
PLANE = NY * NC


def dot(a, b, ca=1, cb=0):
    return lax.dot_general(a, b, (((ca,), (cb,)), ((), ())), preferred_element_type=F32)


def pair_slots(assign_ref, capacity):
    tok = assign_ref.shape[0]
    lane = lax.broadcasted_iota(jnp.int32, (tok, LANES), 1)
    named = [(assign_ref[:, k : k + 1] == lane).astype(F32) for k in range(2)]
    below = (
        lax.broadcasted_iota(jnp.int32, (tok, tok), 0)
        > lax.broadcasted_iota(jnp.int32, (tok, tok), 1)
    ).astype(F32)
    earlier = dot(below.astype(BF16), (named[0] + named[1]).astype(BF16))
    return [
        assign_ref[:, k : k + 1] * capacity
        + jnp.sum(earlier * named[k], axis=1, keepdims=True).astype(jnp.int32)
        for k in range(2)
    ]


def rem(a, n):
    return lax.rem(a, jnp.int32(n))


def div(a, n):
    return lax.div(a, jnp.int32(n))


def rows_at(index, size):
    return pl.ds(pl.multiple_of(index * size, size), size)


def expert_coords():
    me = lax.axis_index("expert").astype(jnp.int32)
    return me, div(me, PLANE), rem(div(me, NC), NY), rem(me, NC)


def expert_peers():
    me, z, y, core = expert_coords()
    out = []
    for dz in (2, 1, 3, 0):
        for dy in (1, 0):
            for dc in (0, 1):
                if (dz, dy, dc) != (0, 0, 0):
                    out.append(
                        rem(z + dz, NZ) * PLANE + rem(y + dy, NY) * NC + rem(core + dc, NC)
                    )
    return out


def layer_kernel(
    capacity,
    chunks,
    partner_ref,
    assign_ref,
    rw_ref,
    tok_ref,
    og_ref,
    w_hbm,
    m_ref,
    v_ref,
    moe_ref,
    tg_ref,
    route_ref,
    moved,
    scaled,
    send_rows,
    send_grads,
    rows_in,
    grads_in,
    w,
    coef_gate,
    coef_up,
    hidden,
    gate_grad,
    up_grad,
    pg,
    ret_eo,
    ret_rg,
    one_l,
    one_r,
    two_l,
    two_r,
    y_in,
    *rest,
):
    count = len(chunks)
    stages, mids = rest[:count], rest[count : 2 * count]
    (
        w_sem,
        rows_s,
        rows_r,
        grads_s,
        grads_r,
        eo_s,
        eo_r,
        rg_s,
        rg_r,
        x_s,
        x_r,
        y_s,
        y_r,
        out_s,
        out_r,
        home_s,
        home_r,
    ) = rest[2 * count :]
    me, z, y, core = expert_coords()
    d = lax.axis_index("dp").astype(jnp.int32)
    x, yl = div(d, 2), rem(d, 2)
    xp, xm, xo = rem(x + 1, NX), rem(x + NX - 1, NX), rem(x + 2, NX)
    right, left, beside = {"dp": xp * 2 + yl}, {"dp": xm * 2 + yl}, {"dp": x * 2 + 1 - yl}
    tok, width = tok_ref.shape
    experts = stages[0].shape[0]
    half = m_ref.shape[2]
    chunk = PLANE * capacity
    peers = expert_peers()
    barrier = pltpu.get_barrier_semaphore()
    for target in [{"expert": peer} for peer in peers] + [right, left, beside]:
        pl.semaphore_signal(barrier, inc=1, device_id=target, device_id_type=MESH)
    w_copies = [pltpu.make_async_copy(w_hbm.at[0, p], w.at[p], w_sem.at[p]) for p in range(3)]
    for copy in w_copies:
        copy.start()

    slot = pair_slots(assign_ref, capacity)
    slot_lane = lax.broadcasted_iota(jnp.int32, (tok, chunk), 1)

    def put(src, dst, sem_s, sem_r, target):
        return pltpu.make_async_remote_copy(
            src_ref=src,
            dst_ref=dst,
            send_sem=sem_s,
            recv_sem=sem_r,
            device_id=target,
            device_id_type=MESH,
        )

    class Swap:
        def __init__(self, source, target, sems_s, sems_r, base=0):
            self.source, self.target = source, target
            self.sems_s, self.sems_r, self.base = sems_s, sems_r, base

        def send(self, peer):
            return put(
                self.source(peer),
                self.target(me),
                self.sems_s.at[self.base + peer],
                self.sems_r.at[self.base + me],
                {"expert": peer},
            )

        def come(self, peer):
            return put(
                self.source(peer),
                self.target(peer),
                self.sems_s.at[self.base + peer],
                self.sems_r.at[self.base + peer],
                {"expert": peer},
            )

        def own(self):
            return pltpu.make_async_copy(
                self.source(me), self.target(me), self.sems_r.at[self.base + me]
            )

        def start(self):
            for peer in peers:
                self.send(peer).start()
            self.own().start()

        def sent(self):
            for peer in peers:
                self.send(peer).wait_send()

        def all_in(self):
            for peer in peers:
                self.come(peer).wait_recv()
            self.own().wait()

    def blocks(ref):
        return lambda e: ref.at[rows_at(e, capacity)]

    swap_rows = Swap(blocks(send_rows), blocks(rows_in), rows_s, rows_r)
    swap_grads = Swap(blocks(send_grads), blocks(grads_in), grads_s, grads_r)
    eo, rg = send_rows, send_grads
    swap_eo = Swap(blocks(eo), blocks(ret_eo), eo_s, eo_r)
    swap_rg = Swap(blocks(rg), blocks(ret_rg), rg_s, rg_r)

    def onehots(plane):
        return [(slot[k] - plane * chunk == slot_lane).astype(F32).astype(BF16) for k in range(2)]

    first = True
    at = 0
    for dz in (2, 1, 3, 0):
        plane = rem(z + dz, NZ)
        hot = onehots(plane)
        send_rows[rows_at(plane, chunk), :] = dot(hot[0] + hot[1], tok_ref[...], 0, 0).astype(BF16)
        if first:
            pl.semaphore_wait(barrier, len(peers) + 3)
            first = False
        number = PLANE - (dz == 0)
        for peer in peers[at : at + number]:
            swap_rows.send(peer).start()
        at += number
    swap_rows.own().start()
    for k in range(2):
        scaled[k * tok : (k + 1) * tok, :] = (
            rw_ref[:, k : k + 1] * og_ref[...].astype(F32)
        ).astype(BF16)
    at = 0
    for dz in (2, 1, 3, 0):
        plane = rem(z + dz, NZ)
        hot = jnp.concatenate(onehots(plane), axis=0)
        send_grads[rows_at(plane, chunk), :] = dot(hot, scaled[...], 0, 0).astype(BF16)
        number = PLANE - (dz == 0)
        for peer in peers[at : at + number]:
            swap_grads.send(peer).start()
        at += number
    swap_grads.own().start()

    for copy in w_copies:
        copy.wait()

    def plane_of(step):
        return rem(z + step + div(step, 2) * (1 - 2 * rem(step, 2)), NZ)

    def forward(step, carry):
        plane = plane_of(step)
        for j in range(PLANE):
            swap_rows.come(plane * PLANE + j).wait_recv()
        at_rows = rows_at(plane, chunk)
        rows = rows_in[at_rows, :]
        gate = dot(rows, w[0])
        up = dot(rows, w[1])
        sig = jax.nn.sigmoid(gate)
        silu = gate * sig
        hidden[at_rows, :] = (silu * up).astype(BF16)
        coef_up[at_rows, :] = silu
        coef_gate[at_rows, :] = up * sig * (1.0 + gate * (1.0 - sig))
        return carry

    lax.fori_loop(0, NZ, forward, 0)
    swap_rows.sent()

    def forward_out(step, carry):
        at_rows = rows_at(step, chunk)
        eo[at_rows, :] = dot(hidden[at_rows, :], w[2], 1, 1).astype(BF16)
        return carry

    lax.fori_loop(0, NZ, forward_out, 0)

    def backward(step, carry):
        plane = plane_of(step)
        for j in range(PLANE):
            swap_grads.come(plane * PLANE + j).wait_recv()
        at_rows = rows_at(plane, chunk)
        hidden_grad = dot(grads_in[at_rows, :], w[2])
        gate_grad[at_rows, :] = (hidden_grad * coef_gate[at_rows, :]).astype(BF16)
        up_grad[at_rows, :] = (hidden_grad * coef_up[at_rows, :]).astype(BF16)
        return carry

    lax.fori_loop(0, NZ, backward, 0)
    swap_eo.start()

    def shard(p, xx, h, cols):
        return pg.at[p, rows_at(xx * 2 + h, half), cols]

    early, late, across = [], [], []
    for i, (p, c0, nc) in enumerate(chunks):
        cols = pl.ds(c0, nc)
        sems = [(x_s.at[6 * i + j], x_r.at[6 * i + j]) for j in range(6)]
        early.append(
            (
                put(shard(p, xo, 0, cols), one_l.at[p, :, cols], *sems[0], right),
                put(shard(p, xo, 1, cols), one_r.at[p, :, cols], *sems[1], left),
                put(shard(p, xp, 1, cols), two_l.at[p, 1, :, cols], *sems[2], right),
                put(shard(p, xm, 0, cols), two_r.at[p, 0, :, cols], *sems[3], left),
            )
        )
        late.append(
            (
                put(one_l.at[p, :, cols], two_l.at[p, 0, :, cols], *sems[4], right),
                put(one_r.at[p, :, cols], two_r.at[p, 1, :, cols], *sems[5], left),
            )
        )
        across.append(
            put(two_l.at[p, 1 - yl, :, cols], y_in.at[p, :, cols], y_s.at[i], y_r.at[i], beside)
        )
    tile = 256

    def weight_grad(p, lhs, rhs):
        def weight_tile(j, carry):
            at_cols = rows_at(j, tile)
            pg[p, at_cols, :] = dot(lhs[:, at_cols], rhs[...], 0, 0).astype(BF16)
            return carry

        lax.fori_loop(0, width // tile, weight_tile, 0)

    def start(group):
        for copy in group:
            copy.start()

    def arrived(group):
        for copy in group:
            copy.wait_recv()

    block = 32
    steps = half // block

    def rows_of(shard_index, i):
        return pl.ds(pl.multiple_of(shard_index * half + i * block, block), block)

    def pass_on(c):
        p, c0, nc = chunks[c]
        cols = pl.ds(c0, nc)

        def add(i, carry):
            at = rows_at(i, block)
            one_l[p, at, cols] = (
                one_l[p, at, cols].astype(F32) + pg[p, rows_of(xp * 2, i), cols].astype(F32)
            ).astype(BF16)
            one_r[p, at, cols] = (
                one_r[p, at, cols].astype(F32) + pg[p, rows_of(xm * 2 + 1, i), cols].astype(F32)
            ).astype(BF16)
            return carry

        lax.fori_loop(0, steps, add, 0)
        start(late[c])

    def give_other(c):
        p, c0, nc = chunks[c]
        cols = pl.ds(c0, nc)
        other = 1 - yl

        def sum_other(i, carry):
            at = rows_at(i, block)
            two_l[p, other, at, cols] = (
                pg[p, rows_of(x * 2 + other, i), cols].astype(F32)
                + two_l[p, other, at, cols].astype(F32)
                + two_r[p, other, at, cols].astype(F32)
            ).astype(BF16)
            return carry

        lax.fori_loop(0, steps, sum_other, 0)
        across[c].start()

    sixteenth = half // experts

    def at_ref(ref):
        return lambda e: ref.at[e]

    def at_home(c):
        p, c0, nc = chunks[c]
        return lambda e: moved.at[p, e, :, :, pl.ds(c0, nc)]

    spread = [
        Swap(at_ref(stages[c]), at_ref(mids[c]), out_s, out_r, c * experts) for c in range(count)
    ]
    settle = [
        Swap(at_ref(stages[c]), at_home(c), home_s, home_r, c * experts) for c in range(count)
    ]

    def update(c):
        p, c0, nc = chunks[c]
        cols = pl.ds(c0, nc)
        across[c].wait_recv()

        def adamw(k, carry):
            at = rows_at(k, sixteenth)
            at_own = pl.ds(pl.multiple_of(d * half + k * sixteenth, sixteenth), sixteenth)
            at_part = pl.ds(
                pl.multiple_of((x * 2 + yl) * half + k * sixteenth, sixteenth), sixteenth
            )
            grad = (
                pg[p, at_part, cols].astype(F32)
                + two_l[p, yl, at, cols].astype(F32)
                + two_r[p, yl, at, cols].astype(F32)
                + y_in[p, at, cols].astype(F32)
            )
            first_new = beta_first * m_ref[0, p, at, cols].astype(F32) + (1.0 - beta_first) * grad
            second_new = (
                beta_second * v_ref[0, p, at, cols].astype(F32) + (1.0 - beta_second) * grad * grad
            )
            full = w[p, at_own, cols].astype(F32)
            change = (
                first_new * (1.0 / first_fix)
                / (jnp.sqrt(second_new * (1.0 / second_fix)) + adam_epsilon)
                + weight_decay * full
            )
            stages[c][k, 0] = (full - learn_rate * change).astype(BF16)
            stages[c][k, 1] = first_new.astype(BF16)
            stages[c][k, 2] = second_new.astype(BF16)
            return carry

        lax.fori_loop(0, experts, adamw, 0)
        spread[c].start()

    def turn(c):
        spread[c].all_in()
        spread[c].sent()

        def reorder(t, carry):
            stages[c][t] = mids[c][partner_ref[t]]
            return carry

        lax.fori_loop(0, experts, reorder, 0)
        settle[c].start()

    slots = ret_eo.shape[0]
    all_lane = lax.broadcasted_iota(jnp.int32, (tok, slots), 1)
    wide = 512

    def hots():
        return [(slot[k] == all_lane).astype(F32).astype(BF16) for k in range(2)]

    def combine_out():
        swap_eo.all_in()
        hot = jnp.concatenate(hots(), axis=0)
        rw = [rw_ref[:, k : k + 1] for k in range(2)]

        def combine(j, route):
            at = rows_at(j, wide)
            pairs = dot(hot, ret_eo[:, at])
            one, two = pairs[:tok], pairs[tok:]
            moe_ref[:, at] = (rw[0] * one + rw[1] * two).astype(BF16)
            grad = og_ref[:, at].astype(F32)
            return (
                route[0] + jnp.sum(grad * one, axis=1, keepdims=True),
                route[1] + jnp.sum(grad * two, axis=1, keepdims=True),
            )

        zero = jnp.zeros((tok, 1), F32)
        route = lax.fori_loop(0, width // wide, combine, (zero, zero))
        route_ref[:, 0:1] = route[0]
        route_ref[:, 1:2] = route[1]

    def combine_grads():
        swap_rg.all_in()
        hot = hots()
        hot_sum = hot[0] + hot[1]

        def combine(j, carry):
            at = rows_at(j, wide)
            tg_ref[:, at] = dot(hot_sum, ret_rg[:, at]).astype(BF16)
            return carry

        lax.fori_loop(0, width // wide, combine, 0)

    weight_grad(2, grads_in, hidden)
    start(early[0])
    start(early[1])
    weight_grad(0, rows_in, gate_grad)
    weight_grad(1, rows_in, up_grad)
    swap_grads.sent()

    def row_tile(j, carry):
        at_cols = rows_at(j, tile)
        rg[:, at_cols] = (
            dot(gate_grad[...], w[0, at_cols, :], 1, 1) + dot(up_grad[...], w[1, at_cols, :], 1, 1)
        ).astype(BF16)
        return carry

    lax.fori_loop(0, width // tile, row_tile, 0)
    swap_rg.start()

    for i in range(count + 3):
        if i < count:
            arrived(early[i])
            if i + 2 < count:
                start(early[i + 2])
            pass_on(i)
        if 0 <= i - 1 < count:
            arrived(late[i - 1])
            give_other(i - 1)
        if 0 <= i - 2 < count:
            update(i - 2)
        if i == 2:
            combine_out()
        if i == 4:
            combine_grads()
        if 0 <= i - 3 < count:
            turn(i - 3)
    for c in range(count):
        settle[c].all_in()
    for c in range(count):
        settle[c].sent()
        for copy in (*early[c], *late[c], across[c]):
            copy.wait_send()
    swap_eo.sent()
    swap_rg.sent()


def per_device(
    tokens, route_weights, assignment, out_grad, weights, first_moment, second_moment, partner
):
    experts = lax.axis_size("expert")
    tok, topk = assignment.shape
    width = tokens.shape[1]
    capacity = 2 * tok * topk // experts
    slots = experts * capacity
    ff = weights.shape[3]
    half = first_moment.shape[2]
    vmem = pl.BlockSpec(memory_space=pltpu.VMEM)
    anywhere = pl.BlockSpec(memory_space=pl.ANY)
    dma = pltpu.SemaphoreType.DMA
    shape = jax.ShapeDtypeStruct
    piece = (3, half, ff)
    sixteenth = half // experts
    cut = ff // 2
    chunks = tuple((p, c0, cut) for p in (2, 0, 1) for c0 in (0, cut))
    sides = [pltpu.VMEM((experts, 3, sixteenth, nc), BF16) for _, _, nc in chunks]
    count = len(chunks)
    wide = pltpu.VMEM((slots, width), BF16)
    moe_out, token_grads, route_grads, moved = pl.pallas_call(
        functools.partial(layer_kernel, capacity, chunks),
        out_shape=(
            shape((tok, width), BF16),
            shape((tok, width), BF16),
            shape((tok, topk), F32),
            shape((3, experts, 3, sixteenth, ff), BF16),
        ),
        in_specs=[pl.BlockSpec(memory_space=pltpu.SMEM)] + [vmem] * 4 + [anywhere] + [vmem] * 2,
        out_specs=(vmem, vmem, vmem, anywhere),
        scratch_shapes=[
            pltpu.VMEM((topk * tok, width), BF16),
            wide,
            wide,
            wide,
            wide,
            pltpu.VMEM((3, width, ff), BF16),
            pltpu.VMEM((slots, ff), F32),
            pltpu.VMEM((slots, ff), F32),
            pltpu.VMEM((slots, ff), BF16),
            pltpu.VMEM((slots, ff), BF16),
            pltpu.VMEM((slots, ff), BF16),
            pltpu.VMEM((3, width, ff), BF16),
            wide,
            wide,
            pltpu.VMEM(piece, BF16),
            pltpu.VMEM(piece, BF16),
            pltpu.VMEM((3, 2, half, ff), BF16),
            pltpu.VMEM((3, 2, half, ff), BF16),
            pltpu.VMEM(piece, BF16),
            *sides,
            *sides,
            dma((3,)),
            *[dma((experts,))] * 8,
            dma((6 * count,)),
            dma((6 * count,)),
            dma((count,)),
            dma((count,)),
            *[dma((count * experts,))] * 4,
        ],
        compiler_params=pltpu.CompilerParams(
            collective_id=0, has_side_effects=True, vmem_limit_bytes=62 * 2**20
        ),
    )(
        partner,
        assignment,
        route_weights,
        tokens,
        out_grad,
        weights,
        first_moment,
        second_moment,
    )
    new = [moved[:, :, k].reshape((1,) + piece) for k in range(3)]
    return (moe_out, token_grads, route_grads, *new)


def solution(mesh):
    placed = (
        P(("expert", "dp"), None),
        P(("expert", "dp"), None),
        P(("expert", "dp"), None),
        P(("expert", "dp"), None),
        P("expert", None, None, None),
        P("expert", None, "dp", None),
        P("expert", None, "dp", None),
        P(),
    )
    return jax.shard_map(
        per_device,
        mesh=mesh,
        in_specs=placed,
        out_specs=(
            P(("expert", "dp"), None),
            P(("expert", "dp"), None),
            P(("expert", "dp"), None),
            P("expert", None, "dp", None),
            P("expert", None, "dp", None),
            P("expert", None, "dp", None),
        ),
        check_vma=False,
    )
```

time: 630 us -> 229 us (0.36)
  waiting for transfers between devices: 452 us -> 0 us
  Pallas kernels: 0 us -> 218 us
  blocking collectives: 37.5 us -> 0 us
  other arithmetic: 35.2 us -> 0 us
  matrix products: 33 us -> 0 us
  starting transfers between devices: 28.5 us -> 0 us
  local copies, waits for them, and re-layouts: 24.3 us -> 10.2 us
  between operations: 14.7 us -> 0.64 us
    pallas_call x0 -> x1, Pallas kernels: none -> 218 us  [per_device(): pl.pallas_call(functools.partial(layer_kernel, capacity, chunks), out_sha...]
    reduce_scatter x1 -> x0, waiting for transfers between devices: 187 us -> none  [per_device(): lax.psum_scatter(partial_grads.astype(jnp.bfloat16), 'dp', scatter_dimens...]
    ppermute x4 -> x0, waiting for transfers between devices: 157 us -> none  [swapped(): lax.ppermute(shard, axis, [(i, i ^ 1 << distance) for i in range(lax.axis...]
    all_to_all x3 -> x0, waiting for transfers between devices: 108 us -> none  [the longest x1 84.7 us: per_device(): lax.all_to_all(row_grads.reshape(loop_size, capacity, width), 'expert', s...]
    all_to_all x1 -> x0, blocking collectives: 37.5 us -> none  [per_device(): lax.all_to_all(send_grads, 'expert', split_axis=0, concat_axis=0, tiled=T...]
    dot_general x9 -> x0, matrix products: 33 us -> none  [the longest x1 5.49 us: per_device(): jnp.dot(grad_flat, weight[2], preferred_element_type=jnp.float32)]
    all_to_all x3 -> x0, starting transfers between devices: 20.7 us -> none  [the longest x1 8.21 us: per_device(): lax.all_to_all(row_grads.reshape(loop_size, capacity, width), 'expert', s...]
    gather x5 -> x0, local copies, waits for them, and re-layouts: 14.9 us -> none  [the longest x1 4.22 us: per_device(): back_grads.reshape(-1, width)[slots].reshape(tok_count, topk_count, width)]
  transfers between devices with their start and end apart: 8 -> 0, of which waited for: 7 -> 0; matrix products, arithmetic and copies ran while one was open for 7% -> 0% of each run, Pallas kernels for 0% -> 0%
where the time goes in v2:
time: 229 us
  Pallas kernels  218 us (95%)
  local copies, waits for them, and re-layouts  10.2 us (4%)
    pallas_call x1, Pallas kernels, per_device(): pl.pallas_call(functools.partial(layer_kernel, capacity, chunks), out_sha...  218 us
    unnamed x9, local copies, waits for them, and re-layouts  6.33 us

profile of v2, /device:TPU:1, one launch (start us, length us, event | category | flops | bytes accessed | tf_op | source)
XLA Modules:
  0.0 228.6 jit_solution(16151008871166348538)
XLA Ops:
  0.6 1.4 copy.15.rw_ref
  2.0 1.4 copy.14.assign_ref
  3.5 217.7 %shard_map.127 = (bf16[128,2048]{1,0:T(8,128)(2,1)}, bf16[128,2048]{1,0:T(8,128)(2,1)}, f32[128,2]{1,0:T(8,128)}, bf16[3,16,3,16,768]{4,3,2,1,0:T(8,128)(2,1)}) custom-call(s32[16]{0:T(128)} %partner_ref.1, s32[128,2]{1,0:T(8,128)} %copy.14.assign_ref, f32[128,2]{1,0:T(8,128)} %copy.15.rw_ref, bf16[128,2048]{1,0:T(8,128)(2,1)} %tok_ref.1, ...), custom_call_target="tpu_custom_call" | custom-call | tf_op jit(solution)/shard_map/pallas_call | solution.py:540
  221.1 1.5 copy.16
  222.6 0.0 copy-start.1
  222.6 3.9 %fusion = (bf16[3,16,1,16,768]{4,3,2,1,0:T(8,128)(2,1)}, bf16[3,16,1,16,768]{4,3,2,1,0:T(8,128)(2,1)}, bf16[3,16,1,16,768]{4,3,2,1,0:T(8,128)(2,1)}) fusion(bf16[3,16,3,16,768]{4,3,2,1,0:T(8,128)(2,1)} %get-tuple-element.13), kind=kLoop, calls=%fused_computation | loop fusion | bytes 7077888 | tf_op jit(solution)/shard_map/slice | solution.py:593
  226.5 0.0 copy-start
  226.5 0.0 copy-done.1
  226.5 0.8 copy.19
  227.3 0.4 copy-done
  227.8 0.8 copy.20
Async XLA Ops:
  222.6 3.9 %copy-start.1 = (bf16[128,2048]{1,0:T(8,128)(2,1)S(1)}, bf16[128,2048]{1,0:T(8,128)(2,1)}, u32[]{:S(2)}) copy-start(bf16[128,2048]{1,0:T(8,128)(2,1)} %get-tuple-element.29) | copy-start | bytes 1572868
  226.5 1.2 copy-start

commit v3 on v2

--- a/solution.py
+++ b/solution.py
@@ -28,17 +28,17 @@
     return lax.dot_general(a, b, (((ca,), (cb,)), ((), ())), preferred_element_type=F32)
 
 
-def pair_slots(assign_ref, capacity):
-    tok = assign_ref.shape[0]
+def pair_slots(assigned, capacity):
+    tok = assigned[0].shape[0]
     lane = lax.broadcasted_iota(jnp.int32, (tok, LANES), 1)
-    named = [(assign_ref[:, k : k + 1] == lane).astype(F32) for k in range(2)]
+    named = [(assigned[k] == lane).astype(F32) for k in range(2)]
     below = (
         lax.broadcasted_iota(jnp.int32, (tok, tok), 0)
         > lax.broadcasted_iota(jnp.int32, (tok, tok), 1)
     ).astype(F32)
     earlier = dot(below.astype(BF16), (named[0] + named[1]).astype(BF16))
     return [
-        assign_ref[:, k : k + 1] * capacity
+        assigned[k] * capacity
         + jnp.sum(earlier * named[k], axis=1, keepdims=True).astype(jnp.int32)
         for k in range(2)
     ]
@@ -78,13 +78,12 @@
     capacity,
     chunks,
     partner_ref,
-    assign_ref,
-    rw_ref,
+    pair_ref,
     tok_ref,
     og_ref,
     w_hbm,
-    m_ref,
-    v_ref,
+    m_hbm,
+    v_hbm,
     moe_ref,
     tg_ref,
     route_ref,
@@ -108,6 +107,8 @@
     two_l,
     two_r,
     y_in,
+    m_ref,
+    v_ref,
     *rest,
 ):
     count = len(chunks)
@@ -138,17 +139,20 @@
     right, left, beside = {"dp": xp * 2 + yl}, {"dp": xm * 2 + yl}, {"dp": x * 2 + 1 - yl}
     tok, width = tok_ref.shape
     experts = stages[0].shape[0]
-    half = m_ref.shape[2]
+    half = m_ref.shape[1]
     chunk = PLANE * capacity
     peers = expert_peers()
     barrier = pltpu.get_barrier_semaphore()
     for target in [{"expert": peer} for peer in peers] + [right, left, beside]:
         pl.semaphore_signal(barrier, inc=1, device_id=target, device_id_type=MESH)
     w_copies = [pltpu.make_async_copy(w_hbm.at[0, p], w.at[p], w_sem.at[p]) for p in range(3)]
+    w_copies.append(pltpu.make_async_copy(m_hbm.at[0], m_ref, w_sem.at[3]))
+    w_copies.append(pltpu.make_async_copy(v_hbm.at[0], v_ref, w_sem.at[4]))
     for copy in w_copies:
         copy.start()
 
-    slot = pair_slots(assign_ref, capacity)
+    rw = [pair_ref[:, k : k + 1] for k in range(2)]
+    slot = pair_slots([pair_ref[:, k + 2 : k + 3].astype(jnp.int32) for k in range(2)], capacity)
     slot_lane = lax.broadcasted_iota(jnp.int32, (tok, chunk), 1)
 
     def put(src, dst, sem_s, sem_r, target):
@@ -231,61 +235,42 @@
     swap_rows.own().start()
     for k in range(2):
         scaled[k * tok : (k + 1) * tok, :] = (
-            rw_ref[:, k : k + 1] * og_ref[...].astype(F32)
+            rw[k] * og_ref[...].astype(F32)
         ).astype(BF16)
-    at = 0
-    for dz in (2, 1, 3, 0):
-        plane = rem(z + dz, NZ)
-        hot = jnp.concatenate(onehots(plane), axis=0)
-        send_grads[rows_at(plane, chunk), :] = dot(hot, scaled[...], 0, 0).astype(BF16)
-        number = PLANE - (dz == 0)
-        for peer in peers[at : at + number]:
-            swap_grads.send(peer).start()
-        at += number
-    swap_grads.own().start()
+    for dz in range(NZ):
+        hot = jnp.concatenate(onehots(dz), axis=0)
+        send_grads[dz * chunk : (dz + 1) * chunk, :] = dot(hot, scaled[...], 0, 0).astype(BF16)
 
     for copy in w_copies:
         copy.wait()
 
-    def plane_of(step):
-        return rem(z + step + div(step, 2) * (1 - 2 * rem(step, 2)), NZ)
-
-    def forward(step, carry):
-        plane = plane_of(step)
-        for j in range(PLANE):
-            swap_rows.come(plane * PLANE + j).wait_recv()
-        at_rows = rows_at(plane, chunk)
-        rows = rows_in[at_rows, :]
-        gate = dot(rows, w[0])
-        up = dot(rows, w[1])
+    swap_rows.all_in()
+    swap_grads.start()
+    ffs = w.shape[2]
+    tile = 256
+
+    def forward(j, carry):
+        at_cols = rows_at(j, tile)
+        rows = rows_in[...]
+        gate = dot(rows, w[0, :, at_cols])
+        up = dot(rows, w[1, :, at_cols])
         sig = jax.nn.sigmoid(gate)
         silu = gate * sig
-        hidden[at_rows, :] = (silu * up).astype(BF16)
-        coef_up[at_rows, :] = silu
-        coef_gate[at_rows, :] = up * sig * (1.0 + gate * (1.0 - sig))
+        hidden[:, at_cols] = (silu * up).astype(BF16)
+        coef_up[:, at_cols] = silu
+        coef_gate[:, at_cols] = up * sig * (1.0 + gate * (1.0 - sig))
         return carry
 
-    lax.fori_loop(0, NZ, forward, 0)
+    lax.fori_loop(0, ffs // tile, forward, 0)
     swap_rows.sent()
 
-    def forward_out(step, carry):
-        at_rows = rows_at(step, chunk)
-        eo[at_rows, :] = dot(hidden[at_rows, :], w[2], 1, 1).astype(BF16)
+    def forward_out(j, carry):
+        at_cols = rows_at(j, tile)
+        eo[:, at_cols] = dot(hidden[...], w[2, at_cols, :], 1, 1).astype(BF16)
         return carry
 
-    lax.fori_loop(0, NZ, forward_out, 0)
-
-    def backward(step, carry):
-        plane = plane_of(step)
-        for j in range(PLANE):
-            swap_grads.come(plane * PLANE + j).wait_recv()
-        at_rows = rows_at(plane, chunk)
-        hidden_grad = dot(grads_in[at_rows, :], w[2])
-        gate_grad[at_rows, :] = (hidden_grad * coef_gate[at_rows, :]).astype(BF16)
-        up_grad[at_rows, :] = (hidden_grad * coef_up[at_rows, :]).astype(BF16)
-        return carry
-
-    lax.fori_loop(0, NZ, backward, 0)
+    lax.fori_loop(0, width // tile, forward_out, 0)
+    swap_grads.all_in()
     swap_eo.start()
 
     def shard(p, xx, h, cols):
@@ -312,7 +297,6 @@
         across.append(
             put(two_l.at[p, 1 - yl, :, cols], y_in.at[p, :, cols], y_s.at[i], y_r.at[i], beside)
         )
-    tile = 256
 
     def weight_grad(p, lhs, rhs):
         def weight_tile(j, carry):
@@ -403,9 +387,9 @@
                 + two_r[p, yl, at, cols].astype(F32)
                 + y_in[p, at, cols].astype(F32)
             )
-            first_new = beta_first * m_ref[0, p, at, cols].astype(F32) + (1.0 - beta_first) * grad
+            first_new = beta_first * m_ref[p, at, cols].astype(F32) + (1.0 - beta_first) * grad
             second_new = (
-                beta_second * v_ref[0, p, at, cols].astype(F32) + (1.0 - beta_second) * grad * grad
+                beta_second * v_ref[p, at, cols].astype(F32) + (1.0 - beta_second) * grad * grad
             )
             full = w[p, at_own, cols].astype(F32)
             change = (
@@ -442,7 +426,6 @@
     def combine_out():
         swap_eo.all_in()
         hot = jnp.concatenate(hots(), axis=0)
-        rw = [rw_ref[:, k : k + 1] for k in range(2)]
 
         def combine(j, route):
             at = rows_at(j, wide)
@@ -474,6 +457,15 @@
 
     weight_grad(2, grads_in, hidden)
     start(early[0])
+
+    def backward(j, carry):
+        at_cols = rows_at(j, tile)
+        hidden_grad = dot(grads_in[...], w[2, :, at_cols])
+        gate_grad[:, at_cols] = (hidden_grad * coef_gate[:, at_cols]).astype(BF16)
+        up_grad[:, at_cols] = (hidden_grad * coef_up[:, at_cols]).astype(BF16)
+        return carry
+
+    lax.fori_loop(0, ffs // tile, backward, 0)
     start(early[1])
     weight_grad(0, rows_in, gate_grad)
     weight_grad(1, rows_in, up_grad)
@@ -489,23 +481,42 @@
     lax.fori_loop(0, width // tile, row_tile, 0)
     swap_rg.start()
 
-    for i in range(count + 3):
-        if i < count:
-            arrived(early[i])
-            if i + 2 < count:
-                start(early[i + 2])
-            pass_on(i)
-        if 0 <= i - 1 < count:
-            arrived(late[i - 1])
-            give_other(i - 1)
-        if 0 <= i - 2 < count:
-            update(i - 2)
-        if i == 2:
-            combine_out()
-        if i == 4:
-            combine_grads()
-        if 0 <= i - 3 < count:
-            turn(i - 3)
+    def first_leg(c):
+        arrived(early[c])
+        if c + 2 < count:
+            start(early[c + 2])
+        pass_on(c)
+
+    def second_leg(c):
+        arrived(late[c])
+        give_other(c)
+
+    first_leg(0)
+    first_leg(1)
+    combine_out()
+    second_leg(0)
+    first_leg(2)
+    second_leg(1)
+    first_leg(3)
+    update(0)
+    second_leg(2)
+    first_leg(4)
+    update(1)
+    turn(0)
+    combine_grads()
+    second_leg(3)
+    first_leg(5)
+    update(2)
+    turn(1)
+    second_leg(4)
+    update(3)
+    turn(2)
+    second_leg(5)
+    update(4)
+    turn(3)
+    update(5)
+    turn(4)
+    turn(5)
     for c in range(count):
         settle[c].all_in()
     for c in range(count):
@@ -545,7 +556,7 @@
             shape((tok, topk), F32),
             shape((3, experts, 3, sixteenth, ff), BF16),
         ),
-        in_specs=[pl.BlockSpec(memory_space=pltpu.SMEM)] + [vmem] * 4 + [anywhere] + [vmem] * 2,
+        in_specs=[pl.BlockSpec(memory_space=pltpu.SMEM)] + [vmem] * 3 + [anywhere] * 3,
         out_specs=(vmem, vmem, vmem, anywhere),
         scratch_shapes=[
             pltpu.VMEM((topk * tok, width), BF16),
@@ -567,9 +578,11 @@
             pltpu.VMEM((3, 2, half, ff), BF16),
             pltpu.VMEM((3, 2, half, ff), BF16),
             pltpu.VMEM(piece, BF16),
+            pltpu.VMEM(piece, BF16),
+            pltpu.VMEM(piece, BF16),
             *sides,
             *sides,
-            dma((3,)),
+            dma((5,)),
             *[dma((experts,))] * 8,
             dma((6 * count,)),
             dma((6 * count,)),
@@ -582,8 +595,7 @@
         ),
     )(
         partner,
-        assignment,
-        route_weights,
+        jnp.concatenate([route_weights, assignment.astype(F32)], axis=1),
         tokens,
         out_grad,
         weights,

time: 229 us -> 227 us (level)
    unnamed x9 -> x7, local copies, waits for them, and re-layouts: 6.33 us -> 3.5 us
where the time goes in v3:
time: 227 us
  Pallas kernels  217 us (96%)
  local copies, waits for them, and re-layouts  8.16 us (4%)
    pallas_call x1, Pallas kernels, per_device(): pl.pallas_call(functools.partial(layer_kernel, capacity, chunks), out_sha...  217 us

profile of v3, /device:TPU:1, one launch (start us, length us, event | category | flops | bytes accessed | tf_op | source)
XLA Modules:
  0.0 226.7 jit_solution(15173957098380298630)
XLA Ops:
  0.6 0.7 convert_element_type.3
  1.3 0.7 pad_maximum_fusion
  2.0 0.7 copy.17.pair_ref
  2.7 216.5 %shard_map.127 = (bf16[128,2048]{1,0:T(8,128)(2,1)}, bf16[128,2048]{1,0:T(8,128)(2,1)}, f32[128,2]{1,0:T(8,128)}, bf16[3,16,3,16,768]{4,3,2,1,0:T(8,128)(2,1)}) custom-call(s32[16]{0:T(128)} %partner_ref.1, f32[128,4]{1,0:T(8,128)} %copy.17.pair_ref, bf16[128,2048]{1,0:T(8,128)(2,1)} %tok_ref.1, bf16[128,2048]{1,0:T(8,128)(2,1)} %og_ref.1, ...), custom_call_target="tpu_custom_call" | custom-call | tf_op jit(solution)/shard_map/pallas_call | solution.py:551
  219.3 1.5 copy.18
  220.7 0.0 copy-start.1
  220.7 3.9 %fusion = (bf16[3,16,1,16,768]{4,3,2,1,0:T(8,128)(2,1)}, bf16[3,16,1,16,768]{4,3,2,1,0:T(8,128)(2,1)}, bf16[3,16,1,16,768]{4,3,2,1,0:T(8,128)(2,1)}) fusion(bf16[3,16,3,16,768]{4,3,2,1,0:T(8,128)(2,1)} %get-tuple-element.13), kind=kLoop, calls=%fused_computation.1 | loop fusion | bytes 7077888 | tf_op jit(solution)/shard_map/slice | solution.py:605
  224.7 0.0 copy-start
  224.7 0.0 copy-done.1
  224.7 0.8 copy.21
  225.5 0.4 copy-done
  225.9 0.8 copy.22
Async XLA Ops:
  220.7 3.9 %copy-start.1 = (bf16[128,2048]{1,0:T(8,128)(2,1)S(1)}, bf16[128,2048]{1,0:T(8,128)(2,1)}, u32[]{:S(2)}) copy-start(bf16[128,2048]{1,0:T(8,128)(2,1)} %get-tuple-element.35) | copy-start | bytes 1572868
  224.7 1.2 copy-start

commit v4 on v3

--- a/solution.py
+++ b/solution.py
@@ -244,8 +244,13 @@
     for copy in w_copies:
         copy.wait()
 
-    swap_rows.all_in()
+    near = len(peers) // 2
+    for peer in peers[near:]:
+        swap_rows.come(peer).wait_recv()
     swap_grads.start()
+    for peer in peers[:near]:
+        swap_rows.come(peer).wait_recv()
+    swap_rows.own().wait()
     ffs = w.shape[2]
     tile = 256
 

time: 227 us -> 227 us (level)
  no operation moved by 1% of the time
where the time goes in v4:
time: 227 us
  Pallas kernels  216 us (95%)
  local copies, waits for them, and re-layouts  8.16 us (4%)
    pallas_call x1, Pallas kernels, per_device(): pl.pallas_call(functools.partial(layer_kernel, capacity, chunks), out_sha...  216 us

profile of v4, /device:TPU:1, one launch (start us, length us, event | category | flops | bytes accessed | tf_op | source)
XLA Modules:
  0.0 226.7 jit_solution(17594874855823128067)
XLA Ops:
  0.6 0.7 convert_element_type.3
  1.3 0.7 pad_maximum_fusion
  2.0 0.7 copy.17.pair_ref
  2.7 216.5 %shard_map.127 = (bf16[128,2048]{1,0:T(8,128)(2,1)}, bf16[128,2048]{1,0:T(8,128)(2,1)}, f32[128,2]{1,0:T(8,128)}, bf16[3,16,3,16,768]{4,3,2,1,0:T(8,128)(2,1)}) custom-call(s32[16]{0:T(128)} %partner_ref.1, f32[128,4]{1,0:T(8,128)} %copy.17.pair_ref, bf16[128,2048]{1,0:T(8,128)(2,1)} %tok_ref.1, bf16[128,2048]{1,0:T(8,128)(2,1)} %og_ref.1, ...), custom_call_target="tpu_custom_call" | custom-call | tf_op jit(solution)/shard_map/pallas_call | solution.py:556
  219.2 1.5 copy.18
  220.7 0.0 copy-start.1
  220.7 3.9 %fusion = (bf16[3,16,1,16,768]{4,3,2,1,0:T(8,128)(2,1)}, bf16[3,16,1,16,768]{4,3,2,1,0:T(8,128)(2,1)}, bf16[3,16,1,16,768]{4,3,2,1,0:T(8,128)(2,1)}) fusion(bf16[3,16,3,16,768]{4,3,2,1,0:T(8,128)(2,1)} %get-tuple-element.13), kind=kLoop, calls=%fused_computation.1 | loop fusion | bytes 7077888 | tf_op jit(solution)/shard_map/slice | solution.py:610
  224.6 0.0 copy-start
  224.6 0.0 copy-done.1
  224.6 0.8 copy.21
  225.4 0.4 copy-done
  225.9 0.8 copy.22
Async XLA Ops:
  220.7 3.9 %copy-start.1 = (bf16[128,2048]{1,0:T(8,128)(2,1)S(1)}, bf16[128,2048]{1,0:T(8,128)(2,1)}, u32[]{:S(2)}) copy-start(bf16[128,2048]{1,0:T(8,128)(2,1)} %get-tuple-element.35) | copy-start | bytes 1572868
  224.6 1.2 copy-start
